TPU v7x, 128 devices: a whole 4x4x4 slice. The times are simulated.
128 devices in a mesh: dp: 8 (over y_hi, z), lib: 16 (over y_lo, x, core).
Axes of the slice: x: 4, y: 4 (y_hi: 2, y_lo: 2; y = y_hi * 2 + y_lo), z: 4, core: 2. Of those that a mesh axis runs over, the one named last changes fastest.
Arguments:
- spectra: bfloat16 [49152, 512], P(('dp', 'lib')), may hold values from -6 to 6
- w_proj: bfloat16 [512, 512], replicated, may hold values from -0.25 to 0.25
- fixed_library_matrix: bfloat16 [16384, 512], P('lib')
- mol_rows: bfloat16 [262144, 512], P(('dp', 'lib'))
- cand_ids: int32 [49152, 4], P(('dp', 'lib')), may hold values from 0 to 262143, as said below
- iso_count: int32 [49152], P(('dp', 'lib')), may hold values from 1 to 3
Outputs:
- grad_w: float32 [512, 512], replicated
- grad_mol: float32 [262144, 512], P(('dp', 'lib'))
- loss: float32 [], replicated
Inputs may be any that keep to these rules, and one draw needn't show every extreme that they name: cand_ids of a spectrum on device dp, lib (in dp+lib order) name rows of the dp group's molecules: id // 2048 // 16 equals dp. Over one device's 1536 slots (all columns, live or not), at most 192 name rows whose (id // 2048) % 16 is one lib index, and exactly 192 for some lib index on every device.
All inputs are finite; a program needn't handle non-finite values.
Results may differ from a plain program's by a relative error of at most 0.0074.
Values may be sent and summed in bfloat16 or wider, within the bound.
A program may use at most 64 MiB of HBM per device.

v0:
```python
import functools

import jax
import jax.numpy as jnp
from jax import lax
from jax.experimental import pallas as pl
from jax.experimental.pallas import tpu as pltpu
from jax.sharding import PartitionSpec as P

F32 = jnp.float32
BF16 = jnp.bfloat16
I32 = jnp.int32
MESH = pl.DeviceIdType.MESH

D = 512
Q = 384
COLS = 4
NLIB = 16
NCHIP = 8
CAP = 192
BANK = 1024
MOL = 2048
CODE_ROWS = 16
ROW_BITS = 11
SLOT_MASK = 2047
OWNER_SHIFT = 22
INV_T = 1.0 / 0.07
PIECE = D // 2 // NLIB
LOG2E = 1.4426950408889634
NSLOTS = NLIB * CAP
PAIR = 2 * CAP


def iota(shape, dim):
    return lax.broadcasted_iota(I32, shape, dim)


def to_row(v):
    eye = iota((128, 128), 0) == iota((128, 128), 1)
    return jnp.concatenate(
        [
            jnp.sum(jnp.where(eye, v[lo : lo + 128], 0.0), axis=0, keepdims=True)
            for lo in range(0, v.shape[0], 128)
        ],
        axis=1,
    )


def to_col(v):
    eye = iota((128, 128), 0) == iota((128, 128), 1)
    return jnp.concatenate(
        [
            jnp.sum(jnp.where(eye, v[:, lo : lo + 128], 0.0), axis=1, keepdims=True)
            for lo in range(0, v.shape[1], 128)
        ],
        axis=0,
    )


def onehot(mask):
    return jnp.where(mask, 1.0, 0.0).astype(BF16)


def dot(a, b):
    return jnp.dot(a, b, preferred_element_type=F32)


def dot_nt(a, b):
    return lax.dot_general(a, b, (((1,), (1,)), ((), ())), preferred_element_type=F32)


def kernel(
    ndp,
    spec_hbm,
    w_hbm,
    bank_hbm,
    mol_hbm,
    ids_ref,
    iso_ref,
    gw_out,
    gm_out,
    loss_out,
    spv,
    gat,
    wv,
    wt,
    bankv,
    bankt,
    molv,
    molt,
    codes,
    posr,
    valr,
    pkt,
    mrow,
    qs,
    unit,
    acc,
    qrow,
    scol,
    stats,
    lse,
    dub,
    gwb,
    rsb,
    dpb,
    dlb,
    ggb,
    loc_sem,
    ids_send,
    ids_recv,
    ag_send,
    ag_recv,
    sb_send,
    sb_recv,
    st_send,
    st_recv,
    rs_send,
    rs_recv,
    dp_send,
    dp_recv,
    dl_send,
    dl_recv,
    gg_send,
    gg_recv,
    out_sem,
):
    dp = lax.axis_index("dp")
    me = lax.axis_index("lib")
    core = lax.rem(me, 2)
    chip = me // 2
    y = chip // 4
    x = lax.rem(chip, 4)

    def chip_at(dy, dx):
        return lax.rem(y + dy, 2) * 4 + lax.rem(x + dx, 4)

    def peer(j):
        return lax.rem(me + j, NLIB)

    def dpeer(j):
        return lax.rem(dp + j, ndp)

    loads = [
        pltpu.make_async_copy(spec_hbm, spv, loc_sem.at[0]),
        pltpu.make_async_copy(w_hbm, wv, loc_sem.at[1]),
        pltpu.make_async_copy(bank_hbm, bankv, loc_sem.at[2]),
        pltpu.make_async_copy(mol_hbm, molv, loc_sem.at[3]),
    ]
    for load in loads:
        load.start()

    barrier = pltpu.get_barrier_semaphore()

    def greet(j, carry):
        pl.semaphore_signal(barrier, inc=1, device_id={"lib": peer(j)}, device_id_type=MESH)
        return carry

    lax.fori_loop(1, NLIB, greet, 0)

    def greet_dp(j, carry):
        pl.semaphore_signal(barrier, inc=1, device_id={"dp": dpeer(j)}, device_id_type=MESH)
        return carry

    lax.fori_loop(1, ndp, greet_dp, 0)
    ids = ids_ref[...]
    column = iota((COLS, Q), 0)
    slot = iota((COLS, Q), 1) * COLS + column
    owner = (ids >> ROW_BITS) & (NLIB - 1)
    code = (owner << OWNER_SHIFT) | ((ids & (MOL - 1)) << ROW_BITS) | slot
    code = jnp.where(column <= iso_ref[...][None, :], code, -1)
    for k in range(Q // 128):
        codes[me, COLS * k : COLS * (k + 1), :] = code[:, 128 * k : 128 * (k + 1)]
    codes[me, Q * COLS // 128 : CODE_ROWS, :] = jnp.full((CODE_ROWS - Q * COLS // 128, 128), -1, I32)
    loads[0].wait()
    gat[chip, :, pl.ds(pl.multiple_of(core * Q, 128), Q)] = spv[...].T
    pl.semaphore_wait(barrier, NLIB - 1 + ndp - 1)

    def ids_copy(j):
        return pltpu.make_async_remote_copy(
            src_ref=codes.at[me],
            dst_ref=codes.at[me],
            send_sem=ids_send.at[j],
            recv_sem=ids_recv.at[me],
            device_id={"lib": peer(j)},
            device_id_type=MESH,
        )

    def ids_from(j):
        s = peer(j)
        return pltpu.make_async_remote_copy(
            src_ref=codes.at[s],
            dst_ref=codes.at[s],
            send_sem=ids_send.at[j],
            recv_sem=ids_recv.at[s],
            device_id={"lib": s},
            device_id_type=MESH,
        )

    lax.fori_loop(1, NLIB, lambda j, c: (ids_copy(j).start(), c)[1], 0)

    def piece(ch, cr, lo, n):
        return gat.at[ch, pl.ds(lo, n), pl.ds(pl.multiple_of(cr * Q, 128), Q)]

    HALF = D // 2
    right = {"lib": chip_at(0, 1) * 2 + core}
    left = {"lib": chip_at(0, 3) * 2 + core}
    across = {"lib": chip_at(1, 0) * 2 + core}
    sibling = {"lib": chip * 2 + 1 - core}

    def ag(idx, dy, dx, lo, n, to):
        ref = piece(chip_at(dy, dx), core, lo, n)
        return pltpu.make_async_remote_copy(
            src_ref=ref, dst_ref=ref, send_sem=ag_send.at[idx], recv_sem=ag_recv.at[idx],
            device_id=to, device_id_type=MESH,
        )

    ag_out = [
        ag(0, 0, 0, 0, D, right),
        ag(1, 0, 0, 0, D, left),
        ag(2, 0, 0, 0, D, across),
        ag(3, 0, 3, 0, HALF, right),
        ag(4, 0, 1, HALF, HALF, left),
        ag(5, 1, 0, 0, D, right),
        ag(6, 1, 0, 0, D, left),
        ag(7, 0, 2, 0, HALF, across),
        ag(8, 0, 2, HALF, HALF, across),
    ]
    arriving = [
        (0, 3, 0, D),
        (0, 1, 0, D),
        (1, 0, 0, D),
        (0, 2, 0, HALF),
        (0, 2, HALF, HALF),
        (1, 3, 0, D),
        (1, 1, 0, D),
        (1, 2, 0, HALF),
        (1, 2, HALF, HALF),
    ]
    ag_in = [ag(k, dy, dx, lo, n, right) for k, (dy, dx, lo, n) in enumerate(arriving)]

    def sb(idx, dy, dx, lo, n, cr):
        ref = piece(chip_at(dy, dx), cr, lo, n)
        return pltpu.make_async_remote_copy(
            src_ref=ref, dst_ref=ref, send_sem=sb_send.at[idx], recv_sem=sb_recv.at[idx],
            device_id=sibling, device_id_type=MESH,
        )

    sb_list = arriving + [(0, 0, 0, D)]
    sb_out = [sb(k, dy, dx, lo, n, core) for k, (dy, dx, lo, n) in enumerate(sb_list)]
    sb_in = [sb(k, dy, dx, lo, n, 1 - core) for k, (dy, dx, lo, n) in enumerate(sb_list)]

    for k in (0, 1, 2):
        ag_out[k].start()
    sb_out[9].start()
    for load in loads[1:]:
        load.wait()
    wt[...] = wv[...].T
    bankt[...] = bankv[...].T
    sb_in[9].wait_recv()

    def compaction():
        lax.fori_loop(1, NLIB, lambda j, c: (ids_from(j).wait_recv(), c)[1], 0)
        n = NLIB * CODE_ROWS
        code = codes[...].reshape(n, 128)
        mine = (code >> OWNER_SHIFT) == me
        ones = onehot(mine)
        before = onehot(iota((128, 128), 0) < iota((128, 128), 1))
        inside = dot(ones, before)
        totals = dot(ones, jnp.ones((128, 128), BF16)).astype(BF16)
        ri, ci = iota((n, n), 0), iota((n, n), 1)
        ahead = onehot((ri // CODE_ROWS == ci // CODE_ROWS) & (ci < ri))
        pos = inside + dot(ahead, totals)
        low = (code & (2**OWNER_SHIFT - 1)) + 1
        posr[...] = jnp.where(mine, pos, -1.0).reshape(NLIB, CODE_ROWS, 128)
        valr[...] = jnp.where(mine, low.astype(F32), 0.0).reshape(NLIB, CODE_ROWS, 128)

        def one(i, carry):
            place = iota((CAP, 128), 0).astype(F32)
            both = []
            for c in (0, 1):
                s = 2 * i + c
                p_all, v_all = posr[s], valr[s]
                total = jnp.zeros((CAP, 128), F32)
                for j in range(Q * COLS // 128):
                    total += jnp.where(p_all[j : j + 1] == place, v_all[j : j + 1], 0.0)
                both.append(jnp.sum(total, axis=1, keepdims=True))
            packed = jnp.concatenate(both, axis=0)
            scol[i, :, 0:1] = packed
            pkt[0:1, pl.ds(pl.multiple_of(i * PAIR, 128), PAIR)] = to_row(packed)
            return carry

        lax.fori_loop(0, NCHIP, one, 0, unroll=4)
        molt[...] = molv[...].T

        def fetch(b, carry):
            lanes = pl.ds(pl.multiple_of(b * 768, 128), 768)
            row = (pkt[0:1, lanes].astype(I32) - 1) >> ROW_BITS
            pick = onehot(row == iota((MOL, 768), 0))
            mrow[:, lanes] = dot(molt[...], pick).astype(BF16)
            return carry

        lax.fori_loop(0, 2, fetch, 0)
        for k in (0, 1, 2):
            ag_in[k].wait_recv()
        for k in (3, 4, 5, 6):
            ag_out[k].start()
        for k in (0, 1, 2):
            sb_out[k].start()
        lax.fori_loop(2, NSLOTS // 768, fetch, 0)

    def bank_unit(ch, kept=None):
        u = dot(wt[...], gat[ch])
        rn = lax.rsqrt(jnp.sum(u * u, axis=0, keepdims=True) + 1e-6)
        u = u * rn
        unit[ch] = u
        qrow[ch, 0:1, :] = rn
        s = dot(bankv[...], u.astype(BF16))
        m = jnp.max(s, axis=0, keepdims=True)
        e = jnp.exp2((s - m) * (INV_T * LOG2E))
        qrow[ch, 1:2, :] = m * INV_T
        qrow[ch, 2:3, :] = jnp.sum(e, axis=0, keepdims=True)
        if kept is None:
            acc[ch] = dot(bankt[...], e.astype(BF16))
        else:
            dub[kept, :] = e.astype(BF16)

    def st_copy(lo, n, j):
        ref = stats.at[me, pl.ds(lo, n)]
        return pltpu.make_async_remote_copy(
            src_ref=ref, dst_ref=ref,
            send_sem=st_send.at[j], recv_sem=st_recv.at[me],
            device_id={"lib": peer(j)}, device_id_type=MESH,
        )

    def st_all(j, s):
        return pltpu.make_async_remote_copy(
            src_ref=stats.at[s], dst_ref=stats.at[s],
            send_sem=st_send.at[j], recv_sem=st_recv.at[s],
            device_id={"lib": peer(j)}, device_id_type=MESH,
        )

    def pair_lanes(i):
        return pl.ds(pl.multiple_of(i * PAIR, 128), PAIR)

    def slot_rows(i):
        t = pkt[0:1, pair_lanes(i)].astype(I32) - 1
        second = jnp.where(iota((1, PAIR), 1) >= CAP, Q, 0)
        q = jnp.where(t < 0, -1, ((t & SLOT_MASK) >> 2) + second)
        return t >= 0, (t >= 0) & ((t & 3) == 0), onehot(q == iota((2 * Q, PAIR), 0))

    def cand_unit(t_order, i):
        lanes = pair_lanes(i)
        _, first, pick = slot_rows(i)
        q_slot = dot(unit[i].astype(BF16), pick)
        qs[:, lanes] = q_slot.astype(BF16)
        cs = jnp.sum(q_slot * mrow[:, lanes].astype(F32), axis=0, keepdims=True) * INV_T
        pkt[1:2, lanes] = cs
        part = jnp.sum(jnp.where(first, cs, 0.0), axis=1, keepdims=True)
        cs_col = to_col(cs)
        for c in (0, 1):
            t = scol[i, c * CAP : (c + 1) * CAP, 0:1].astype(I32) - 1
            q = (t & SLOT_MASK) >> 2
            chosen = jnp.where(q == iota((CAP, Q), 1), cs_col[c * CAP : (c + 1) * CAP], -1e30)
            mb = qrow[i, 1:2, c * Q : (c + 1) * Q]
            lb = qrow[i, 2:3, c * Q : (c + 1) * Q]
            top = jnp.maximum(mb, jnp.max(chosen, axis=0, keepdims=True))
            total = lb * jnp.exp(mb - top) + jnp.sum(jnp.exp(chosen - top), axis=0, keepdims=True)
            out = top + jnp.log(total)
            for k in range(3):
                stats[me, t_order, 3 * c + k : 3 * c + k + 1, :] = out[:, 128 * k : 128 * (k + 1)]
        stats[me, t_order, 6:8, :] = jnp.broadcast_to(part, (2, 128))

    def send_stats(lo, n):
        lax.fori_loop(1, NLIB, lambda j, k: (st_copy(lo, n, j).start(), k)[1], 0)

    def order(t):
        dy = jnp.where((t == 3) | (t >= 5), 1, 0)
        dx = jnp.where(
            (t == 1) | (t == 5), 1, jnp.where((t == 2) | (t == 6), 3, jnp.where((t == 4) | (t == 7), 2, 0))
        )
        return chip_at(dy, dx)

    bank_unit(chip)
    compaction()

    def step(keep, t, carry):
        @pl.when(t == 1)
        def _():
            for k in (1, 0, 2):
                sb_in[k].wait_recv()

        @pl.when(t == 3)
        def _():
            for k in (3, 4):
                ag_in[k].wait_recv()
            for k in (7, 8):
                ag_out[k].start()
            for k in (3, 4):
                sb_out[k].start()

        @pl.when(t == 4)
        def _():
            for k in (3, 4):
                sb_in[k].wait_recv()
            for k in (5, 6):
                ag_in[k].wait_recv()
            for k in (5, 6):
                sb_out[k].start()

        @pl.when(t == 5)
        def _():
            for k in (5, 6):
                sb_in[k].wait_recv()

        @pl.when(t == 6)
        def _():
            for k in (7, 8):
                ag_in[k].wait_recv()
            for k in (7, 8):
                sb_out[k].start()

        @pl.when(t == 7)
        def _():
            for k in (7, 8):
                sb_in[k].wait_recv()

        cand_unit(t - 1, order(t - 1))
        bank_unit(order(t), kept_rows(t) if keep else None)
        return carry

    def kept_rows(t):
        return pl.ds(pl.multiple_of((t - 4) * BANK, BANK), BANK)

    lax.fori_loop(1, 4, functools.partial(step, False), 0)
    lax.fori_loop(4, 5, functools.partial(step, True), 0)
    send_stats(0, 4)
    lax.fori_loop(5, NCHIP, functools.partial(step, True), 0)
    send_stats(4, 3)
    cand_unit(NCHIP - 1, chip_at(1, 2))
    send_stats(NCHIP - 1, 1)

    def kept_sum(t, carry):
        acc[order(t)] = dot(bankt[...], dub[kept_rows(t), :])
        return carry

    lax.fori_loop(4, NCHIP, kept_sum, 0)

    lax.fori_loop(1, NLIB, lambda j, k: (st_all(j, peer(j)).wait_recv(), k)[1], 0)

    place = {(0, 0): 0, (0, 1): 1, (0, 3): 2, (1, 0): 3, (0, 2): 4, (1, 1): 5, (1, 3): 6, (1, 2): 7}
    values, firsts = [], []
    for i in range(NCHIP):
        parts = []
        for s in range(NLIB):
            dy, dx = (i // 4 + s // 8) % 2, (i % 4 - s // 2 % 4) % 4
            parts.append(stats[s, place[dy, dx]])
        top = parts[0]
        for part in parts[1:]:
            top = jnp.maximum(top, part)
        total = jnp.exp(parts[0] - top)
        first_score = parts[0]
        for part in parts[1:]:
            total += jnp.exp(part - top)
            first_score += part
        one_value = top + jnp.log(total)
        lse[i] = one_value
        values.append(one_value)
        firsts.append(first_score)
    value = jnp.stack(values)
    first_scores = jnp.stack(firsts)
    in_row = iota((NCHIP, 8, 128), 1)
    lane0 = iota((NCHIP, 8, 128), 2) == 0
    terms = jnp.where(in_row < 6, value, jnp.where((in_row == 6) & lane0, -first_scores, 0.0))
    terms = jnp.sum(terms, axis=0)
    group_loss = jnp.sum(jnp.sum(terms, axis=1, keepdims=True), axis=0, keepdims=True)
    dlb[dp] = jnp.broadcast_to(group_loss, (8, 128))

    def dl_copy(j, s, to):
        return pltpu.make_async_remote_copy(
            src_ref=dlb.at[s], dst_ref=dlb.at[s], send_sem=dl_send.at[j], recv_sem=dl_recv.at[s],
            device_id={"dp": to}, device_id_type=MESH,
        )


    def grad_unit(i, carry):
        lanes = pair_lanes(i)
        lse_row = jnp.concatenate([lse[i, k : k + 1, :] for k in range(6)], axis=1)
        valid, first, pick = slot_rows(i)
        high = lse_row.astype(BF16).astype(F32)
        middle = (lse_row - high).astype(BF16).astype(F32)
        low = lse_row - high - middle
        thirds = jnp.concatenate([high, middle, low, jnp.zeros((5, 2 * Q), F32)], axis=0)
        thirds = dot(thirds.astype(BF16), pick)
        lse_slot = thirds[0:1] + thirds[1:2] + thirds[2:3]
        coef = jnp.where(
            valid, jnp.exp(pkt[1:2, lanes] - lse_slot) - jnp.where(first, 1.0, 0.0), 0.0
        )
        pkt[2:3, lanes] = coef * INV_T
        weighted = (mrow[:, lanes].astype(F32) * coef).astype(BF16)
        scale = jnp.exp(qrow[i, 1:2, :] - lse_row)
        dq = acc[i] * scale + dot_nt(weighted, pick)
        u = unit[i]
        along = jnp.sum(u * dq, axis=0, keepdims=True)
        du = (dq - u * along) * (qrow[i, 0:1, :] * INV_T)
        dub[pl.ds(pl.multiple_of(i * D, D), D), :] = du.astype(BF16)
        return carry

    lax.fori_loop(0, NCHIP, grad_unit, 0, unroll=2)

    def rs_copy(h, j, src, dst, to):
        return pltpu.make_async_remote_copy(
            src_ref=gwb.at[h, src], dst_ref=rsb.at[h, dst],
            send_sem=rs_send.at[h, j], recv_sem=rs_recv.at[h, dst],
            device_id={"lib": to}, device_id_type=MESH,
        )

    def dp_copy(h, j, s, to):
        return pltpu.make_async_remote_copy(
            src_ref=dpb.at[h, s], dst_ref=dpb.at[h, s],
            send_sem=dp_send.at[h, j], recv_sem=dp_recv.at[h, s],
            device_id={"dp": to}, device_id_type=MESH,
        )

    def gg_copy(h, j, s, to):
        return pltpu.make_async_remote_copy(
            src_ref=ggb.at[h, s], dst_ref=ggb.at[h, s],
            send_sem=gg_send.at[h, j], recv_sem=gg_recv.at[h, s],
            device_id={"lib": to}, device_id_type=MESH,
        )

    def rs_begin(h):
        rows = slice(h * (D // 2), (h + 1) * (D // 2))
        half = dot_nt(gat[0, rows, :], dub[0:D, :])
        for i in range(1, NCHIP):
            half += dot_nt(gat[i, rows, :], dub[i * D : (i + 1) * D, :])
        gwb[h] = half.astype(BF16).reshape(NLIB, PIECE, D)
        lax.fori_loop(1, NLIB, lambda j, k: (rs_copy(h, j, peer(j), me, peer(j)).start(), k)[1], 0)
        rsb[h, me] = gwb[h, me]

    def dp_begin(h):
        lax.fori_loop(1, NLIB, lambda j, k: (rs_copy(h, j, me, peer(j), peer(j)).wait_recv(), k)[1], 0)
        part = rsb[h, 0].astype(F32)
        for s in range(1, NLIB):
            part += rsb[h, s].astype(F32)
        dpb[h, dp] = part.astype(BF16)
        lax.fori_loop(1, ndp, lambda j, k: (dp_copy(h, j, dp, dpeer(j)).start(), k)[1], 0)

    def gg_begin(h):
        lax.fori_loop(1, ndp, lambda j, k: (dp_copy(h, j, dpeer(j), dpeer(j)).wait_recv(), k)[1], 0)
        part = dpb[h, 0].astype(F32)
        for s in range(1, ndp):
            part += dpb[h, s].astype(F32)
        ggb[h, me] = part.astype(BF16)
        lax.fori_loop(1, NLIB, lambda j, k: (gg_copy(h, j, me, peer(j)).start(), k)[1], 0)

    def gg_end(h):
        lax.fori_loop(1, NLIB, lambda j, k: (gg_copy(h, j, peer(j), peer(j)).wait_recv(), k)[1], 0)

    rs_begin(0)
    rs_begin(1)
    lax.fori_loop(1, ndp, lambda j, k: (dl_copy(j, dp, dpeer(j)).start(), k)[1], 0)

    def out_copy(r):
        return pltpu.make_async_copy(
            acc.at[r, pl.ds(0, 256), pl.ds(0, D)],
            gm_out.at[pl.ds(pl.multiple_of(r * 256, 256), 256), :],
            out_sem.at[r],
        )

    def scatter(r, carry):
        row = (pkt[0:1, :].astype(I32) - 1) >> ROW_BITS
        pick = onehot(row == iota((256, NSLOTS), 0) + r * 256)
        acc[r, 0:256, 0:D] = dot_nt(pick, qs[...])
        out_copy(r).start()
        return carry

    def slot_gradients(i, carry):
        lanes = pair_lanes(i)
        qs[:, lanes] = (qs[:, lanes].astype(F32) * pkt[2:3, lanes]).astype(BF16)
        return carry

    lax.fori_loop(0, NCHIP, slot_gradients, 0)
    lax.fori_loop(0, 2, scatter, 0)
    dp_begin(0)
    lax.fori_loop(2, 4, scatter, 0)
    dp_begin(1)
    lax.fori_loop(4, 6, scatter, 0)
    gg_begin(0)
    lax.fori_loop(6, 8, scatter, 0)
    gg_begin(1)

    lax.fori_loop(1, ndp, lambda j, k: (dl_copy(j, dpeer(j), dpeer(j)).wait_recv(), k)[1], 0)
    whole = jnp.zeros((8, 128), F32)
    for s in range(ndp):
        whole += dlb[s]
    loss_out[...] = whole[0:1, 0:1] * (1.0 / (Q * NLIB * ndp))

    gg_end(0)
    gg_end(1)
    gw_out[...] = ggb[...].reshape(D, D)

    lax.fori_loop(1, NLIB, lambda j, k: (st_all(j, me).wait_send(), k)[1], 0)
    lax.fori_loop(0, 8, lambda r, k: (out_copy(r).wait(), k)[1], 0)
    lax.fori_loop(1, NLIB, lambda j, k: (ids_copy(j).wait_send(), k)[1], 0)
    for k in range(9):
        ag_out[k].wait_send()
    for k in range(10):
        sb_out[k].wait_send()
    for h in (0, 1):
        lax.fori_loop(1, NLIB, lambda j, k: (rs_copy(h, j, peer(j), me, peer(j)).wait_send(), k)[1], 0)
        lax.fori_loop(1, NLIB, lambda j, k: (gg_copy(h, j, me, peer(j)).wait_send(), k)[1], 0)
        lax.fori_loop(1, ndp, lambda j, k: (dp_copy(h, j, dp, dpeer(j)).wait_send(), k)[1], 0)
    lax.fori_loop(1, ndp, lambda j, k: (dl_copy(j, dp, dpeer(j)).wait_send(), k)[1], 0)


def per_device(ndp, spectra, w_proj, fixed_library_matrix, mol_rows, cand_ids, iso_count):
    vmem = pl.BlockSpec(memory_space=pltpu.VMEM)
    hbm = pl.BlockSpec(memory_space=pl.ANY)
    dma = pltpu.SemaphoreType.DMA
    gw, gm, loss = pl.pallas_call(
        functools.partial(kernel, ndp),
        out_shape=(
            jax.ShapeDtypeStruct((D, D), BF16),
            jax.ShapeDtypeStruct((MOL, D), F32),
            jax.ShapeDtypeStruct((1, 1), F32),
        ),
        in_specs=[hbm, hbm, hbm, hbm, vmem, vmem],
        out_specs=(vmem, hbm, vmem),
        scratch_shapes=[
            pltpu.VMEM((Q, D), BF16),
            pltpu.VMEM((NCHIP, D, 2 * Q), BF16),
            pltpu.VMEM((D, D), BF16),
            pltpu.VMEM((D, D), BF16),
            pltpu.VMEM((BANK, D), BF16),
            pltpu.VMEM((D, BANK), BF16),
            pltpu.VMEM((MOL, D), BF16),
            pltpu.VMEM((D, MOL), BF16),
            pltpu.VMEM((NLIB, CODE_ROWS, 128), I32),
            pltpu.VMEM((NLIB, CODE_ROWS, 128), F32),
            pltpu.VMEM((NLIB, CODE_ROWS, 128), F32),
            pltpu.VMEM((8, NSLOTS), F32),
            pltpu.VMEM((D, NSLOTS), BF16),
            pltpu.VMEM((D, NSLOTS), BF16),
            pltpu.VMEM((NCHIP, D, 2 * Q), F32),
            pltpu.VMEM((NCHIP, D, 2 * Q), F32),
            pltpu.VMEM((NCHIP, 8, 2 * Q), F32),
            pltpu.VMEM((NCHIP, PAIR, 128), F32),
            pltpu.VMEM((NLIB, NCHIP, 8, 128), F32),
            pltpu.VMEM((NCHIP, 8, 128), F32),
            pltpu.VMEM((NCHIP * D, 2 * Q), BF16),
            pltpu.VMEM((2, NLIB, PIECE, D), BF16),
            pltpu.VMEM((2, NLIB, PIECE, D), BF16),
            pltpu.VMEM((2, ndp, PIECE, D), BF16),
            pltpu.VMEM((ndp, 8, 128), F32),
            pltpu.VMEM((2, NLIB, PIECE, D), BF16),
            dma((4,)),
            dma((NLIB,)),
            dma((NLIB,)),
            dma((9,)),
            dma((9,)),
            dma((10,)),
            dma((10,)),
            dma((NLIB,)),
            dma((NLIB,)),
            dma((2, NLIB)),
            dma((2, NLIB)),
            dma((2, ndp)),
            dma((2, ndp)),
            dma((ndp,)),
            dma((ndp,)),
            dma((2, NLIB)),
            dma((2, NLIB)),
            dma((8,)),
        ],
        compiler_params=pltpu.CompilerParams(
            collective_id=0, has_side_effects=True, vmem_limit_bytes=62 * 1024 * 1024
        ),
    )(spectra, w_proj, fixed_library_matrix, mol_rows, cand_ids.T, iso_count)
    return gw.astype(F32), gm, loss.reshape(())


def solution(mesh):
    placed = (
        P(("dp", "lib"), None),
        P(),
        P("lib", None),
        P(("dp", "lib"), None),
        P(("dp", "lib"), None),
        P(("dp", "lib")),
    )
    return jax.shard_map(
        functools.partial(per_device, mesh.shape["dp"]),
        mesh=mesh,
        in_specs=placed,
        out_specs=(P(), P(("dp", "lib"), None), P()),
        check_vma=False,
    )
```

profile of v0, /device:TPU:1, one launch (start us, length us, event | category | flops | bytes accessed | tf_op | source)
XLA Modules:
  0.0 99.0 jit_solution(15093562540684379974)
XLA Ops:
  0.6 89.8 %shard_map.85 = (bf16[512,512]{1,0:T(8,128)(2,1)}, f32[2048,512]{1,0:T(8,128)}, f32[1,1]{1,0:T(1,128)}) custom-call(bf16[384,512]{1,0:T(8,128)(2,1)} %spec_hbm.1, bf16[512,512]{1,0:T(8,128)(2,1)} %w_hbm.1, bf16[1024,512]{1,0:T(8,128)(2,1)} %bank_hbm.1, bf16[2048,512]{1,0:T(8,128)(2,1)} %mol_hbm.1, s32[4,384]{1,0:T(4,128)} %bitcast.2, s32[384]{0:T(512)} %iso_ref.1), custom_call_target="tpu_custom_call" | custom-call | tf_op jit(solution)/shard_map/pallas_call | solution.py:621
  90.4 2.1 %convert_element_type.3 = f32[512,512]{1,0:T(8,128)} convert(bf16[512,512]{1,0:T(8,128)(2,1)} %get-tuple-element.6) | non-fusion elementwise | flops 262144 | bytes 1572864 | tf_op jit(solution)/shard_map/convert_element_type | solution.py:680
  92.6 4.6 %copy.11 = f32[2048,512]{1,0:T(8,128)} copy(f32[2048,512]{1,0:T(8,128)} %get-tuple-element.13) | data formatting | bytes 8388608
where the time goes:
time: 99.2 us; the launch traced here: 99 us
  Pallas kernels  89.8 us (91%)
  local copies, waits for them, and re-layouts  4.64 us (5%)
  between operations  2.4 us (2%)
  other arithmetic  2.15 us (2%)
    pallas_call x1, Pallas kernels, per_device(): pl.pallas_call(functools.partial(kernel, ndp), out_shape=(jax.ShapeDtypeS...  89.8 us
    unnamed x1, local copies, waits for them, and re-layouts  4.64 us
    convert_element_type x1, other arithmetic, per_device(): return (gw.astype(F32), gm, loss.reshape(()))  2.15 us

commit v1 on v0

--- a/solution.py
+++ b/solution.py
@@ -300,14 +300,14 @@
             mrow[:, lanes] = dot(molt[...], pick).astype(BF16)
             return carry
 
-        lax.fori_loop(0, 2, fetch, 0)
+        lax.fori_loop(0, 2, fetch, 0, unroll=2)
         for k in (0, 1, 2):
             ag_in[k].wait_recv()
         for k in (3, 4, 5, 6):
             ag_out[k].start()
         for k in (0, 1, 2):
             sb_out[k].start()
-        lax.fori_loop(2, NSLOTS // 768, fetch, 0)
+        lax.fori_loop(2, NSLOTS // 768, fetch, 0, unroll=2)
 
     def bank_unit(ch, kept=None):
         u = dot(wt[...], gat[ch])
@@ -444,7 +444,7 @@
         acc[order(t)] = dot(bankt[...], dub[kept_rows(t), :])
         return carry
 
-    lax.fori_loop(4, NCHIP, kept_sum, 0)
+    lax.fori_loop(4, NCHIP, kept_sum, 0, unroll=2)
 
     lax.fori_loop(1, NLIB, lambda j, k: (st_all(j, peer(j)).wait_recv(), k)[1], 0)
 
@@ -581,13 +581,13 @@
         return carry
 
     lax.fori_loop(0, NCHIP, slot_gradients, 0)
-    lax.fori_loop(0, 2, scatter, 0)
+    lax.fori_loop(0, 2, scatter, 0, unroll=2)
     dp_begin(0)
-    lax.fori_loop(2, 4, scatter, 0)
+    lax.fori_loop(2, 4, scatter, 0, unroll=2)
     dp_begin(1)
-    lax.fori_loop(4, 6, scatter, 0)
+    lax.fori_loop(4, 6, scatter, 0, unroll=2)
     gg_begin(0)
-    lax.fori_loop(6, 8, scatter, 0)
+    lax.fori_loop(6, 8, scatter, 0, unroll=2)
     gg_begin(1)
 
     lax.fori_loop(1, ndp, lambda j, k: (dl_copy(j, dpeer(j), dpeer(j)).wait_recv(), k)[1], 0)

time: 99.2 us -> 98.5 us (level)
  no operation moved by 1% of the time
where the time goes in v1:
time: 98.5 us; the launch traced here: 98.3 us
  Pallas kernels  89.1 us (90%)
  local copies, waits for them, and re-layouts  4.64 us (5%)
  between operations  2.4 us (2%)
  other arithmetic  2.15 us (2%)
    pallas_call x1, Pallas kernels, per_device(): pl.pallas_call(functools.partial(kernel, ndp), out_shape=(jax.ShapeDtypeS...  89.1 us
    unnamed x1, local copies, waits for them, and re-layouts  4.64 us
    convert_element_type x1, other arithmetic, per_device(): return (gw.astype(F32), gm, loss.reshape(()))  2.15 us

profile of v1, /device:TPU:1, one launch (start us, length us, event | category | flops | bytes accessed | tf_op | source)
XLA Modules:
  0.0 98.3 jit_solution(3241334140092864346)
XLA Ops:
  0.6 89.1 %shard_map.85 = (bf16[512,512]{1,0:T(8,128)(2,1)}, f32[2048,512]{1,0:T(8,128)}, f32[1,1]{1,0:T(1,128)}) custom-call(bf16[384,512]{1,0:T(8,128)(2,1)} %spec_hbm.1, bf16[512,512]{1,0:T(8,128)(2,1)} %w_hbm.1, bf16[1024,512]{1,0:T(8,128)(2,1)} %bank_hbm.1, bf16[2048,512]{1,0:T(8,128)(2,1)} %mol_hbm.1, s32[4,384]{1,0:T(4,128)} %bitcast.2, s32[384]{0:T(512)} %iso_ref.1), custom_call_target="tpu_custom_call" | custom-call | tf_op jit(solution)/shard_map/pallas_call | solution.py:621
  89.7 2.1 %convert_element_type.3 = f32[512,512]{1,0:T(8,128)} convert(bf16[512,512]{1,0:T(8,128)(2,1)} %get-tuple-element.6) | non-fusion elementwise | flops 262144 | bytes 1572864 | tf_op jit(solution)/shard_map/convert_element_type | solution.py:680
  91.9 4.6 %copy.11 = f32[2048,512]{1,0:T(8,128)} copy(f32[2048,512]{1,0:T(8,128)} %get-tuple-element.13) | data formatting | bytes 8388608
